TPU v7x, 512 devices: a whole 4x4x16 slice. The times are simulated.
512 devices in a mesh: dom: 64 (over x, z), head: 8 (over y, core).
Axes of the slice: x: 4, y: 4, z: 16, core: 2. Of those that a mesh axis runs over, the one named last changes fastest.
Arguments:
- node_feats: bfloat16 [65536, 512], P(('dom', 'head')), may hold values from -6 to 6
- norm_gain: float32 [512], replicated, may hold values from 0.25 to 1.75
- w_qkv: bfloat16 [512, 1536], P(None, 'head'), may hold values from -1 to 1
- w_out: bfloat16 [512, 512], replicated, may hold values from -0.25 to 0.25
- rand_feat: float32 [8, 64, 256], P('head'), may hold values from -6 to 6
- temper: float32 [8], P('head'), may hold values from 1 to 6
- edge_src: int32 [512, 6], P('dom'), may hold values from 0 to 511, as said below
- edge_count: int32 [512], P('dom'), may hold values from 1 to 6, as said below
- block_fill: int32 [512], replicated, may hold values from 32 to 128, as said below
Outputs:
- update: bfloat16 [65536, 512], P(('dom', 'head'))
Inputs may be any that keep to these rules, and one draw needn't show every extreme that they name: `edge_src`: destination block b lies in partition p = b // 8; each of its source blocks lies in partition p - 1, p or p + 1; slot 0 holds b itself, and slots at or beyond edge_count[b] hold b. `edge_count`: every block of some partition uses all 6 slots. `block_fill`: block 0 is full.
All inputs are finite; a program needn't handle non-finite values.
Results may differ from a plain program's by a relative error of at most 0.012.
The roundings to bfloat16 on the way count: a program that leaves them out, or rounds other values in their place, can miss the bound.
Values may be sent and summed in bfloat16 or wider, within the bound.
A program may use at most 64 MiB of HBM per device.

v0:
```python
import math
import jax
import jax.numpy as jnp
from jax import lax
from jax.sharding import PartitionSpec as P

BLK = 128


def padded(block, sides, width):
    for axis, dim in sides:
        count = lax.axis_size(axis)
        forward = [(i, i + 1) for i in range(count - 1)]
        backward = [(target, source) for source, target in forward]
        low = lax.ppermute(
            lax.slice_in_dim(block, block.shape[dim] - width, None, axis=dim), axis, forward
        )
        high = lax.ppermute(lax.slice_in_dim(block, 0, width, axis=dim), axis, backward)
        block = jnp.concatenate([low, block, high], axis=dim)
    return block


def layer_norm(rows, gain):
    widened = rows.astype(jnp.float32)
    centred = widened - jnp.mean(widened, axis=-1, keepdims=True)
    spread = jnp.mean(centred * centred, axis=-1, keepdims=True)
    return (centred * lax.rsqrt(spread + 1e-05) * gain).astype(jnp.bfloat16)


def features(rows, directions, temper):
    head_dim = rows.shape[-1]
    scaled = rows.astype(jnp.float32) * (jnp.sqrt(temper)[None, :, None] * head_dim ** (-0.25))
    lifted = jnp.einsum("nhd,hdm->nhm", scaled, directions, precision=lax.Precision.HIGHEST)
    return jnp.exp(
        lifted - 0.5 * jnp.sum(scaled * scaled, axis=-1, keepdims=True)
    ) * directions.shape[2] ** (-0.5)


def shards(
    node_feats, norm_gain, w_qkv, w_out, rand_feat, temper, edge_src, edge_count, block_fill
):
    groups = lax.axis_size("head")
    heads_here = rand_feat.shape[0]
    head_dim = rand_feat.shape[1]
    part_rows = node_feats.shape[0] * groups
    blocks = part_rows // BLK
    slots = edge_src.shape[1]
    domain = lax.axis_index("dom")
    normed = layer_norm(node_feats, norm_gain)
    qkv = jnp.dot(
        lax.all_gather(normed, "head", axis=0, tiled=True),
        w_qkv,
        preferred_element_type=jnp.float32,
    ).astype(jnp.bfloat16)
    split = qkv.reshape(part_rows, heads_here, 3, head_dim)
    queries = split[:, :, 0]
    own_fill = lax.dynamic_slice_in_dim(block_fill, domain * blocks, blocks)
    lanes = lax.broadcasted_iota(jnp.int32, (blocks, BLK), 1)
    valid = (lanes < own_fill[:, None]).astype(jnp.float32).reshape(part_rows)
    phi_keys = features(split[:, :, 1], rand_feat, temper) * valid[:, None, None]
    partial_sum = jnp.einsum(
        "nhm,nhe->hme",
        phi_keys,
        split[:, :, 2].astype(jnp.float32),
        precision=lax.Precision.HIGHEST,
    )
    kernel_sum, key_total = lax.psum((partial_sum, jnp.sum(phi_keys, axis=0)), "dom")
    pairs = split[:, :, 1:].reshape(part_rows, heads_here * 2 * head_dim)
    widened = padded(pairs, (("dom", 0),), part_rows)
    kv_blocks = widened.reshape(3 * blocks, BLK, heads_here, 2, head_dim)
    key_blocks = kv_blocks[:, :, :, 0]
    value_blocks = kv_blocks[:, :, :, 1]
    local_src = edge_src - (domain - 1) * blocks
    scale = head_dim ** (-0.5)
    per_step = math.gcd(blocks, max(1, 8 // heads_here))
    turns = blocks // per_step
    width = slots * BLK
    q_steps = queries.reshape(turns, per_step, BLK, heads_here, head_dim)
    src_steps = local_src.reshape(turns, per_step, slots)
    id_steps = edge_src.reshape(turns, per_step, slots)
    count_steps = edge_count.reshape(turns, per_step)

    def attend_all(packed):
        q_part, src_part, id_part, count_part = packed
        keys = jnp.take(key_blocks, src_part, axis=0).reshape(per_step, width, heads_here, head_dim)
        values = jnp.take(value_blocks, src_part, axis=0).reshape(
            per_step, width, heads_here, head_dim
        )
        fills = jnp.take(block_fill, id_part)
        slot_ids = lax.broadcasted_iota(jnp.int32, (per_step, slots, BLK), 1)
        lane_ids = lax.broadcasted_iota(jnp.int32, (per_step, slots, BLK), 2)
        allowed = ((lane_ids < fills[:, :, None]) & (slot_ids < count_part[:, None, None])).reshape(
            per_step, width
        )
        scores = (
            jnp.einsum("bqhd,bkhd->bhqk", q_part, keys, preferred_element_type=jnp.float32) * scale
        )
        scores = jnp.where(allowed[:, None, None, :], scores, -1e30)
        row_max = jnp.max(scores, axis=3, keepdims=True)
        weights = jnp.exp(scores - row_max)
        total = jnp.sum(weights, axis=3)
        accum = jnp.einsum(
            "bhqk,bkhd->bqhd",
            weights.astype(jnp.bfloat16),
            values,
            preferred_element_type=jnp.float32,
        )
        return accum / jnp.transpose(total, (0, 2, 1))[..., None]

    local = lax.map(attend_all, (q_steps, src_steps, id_steps, count_steps))
    local = local.reshape(part_rows, heads_here, head_dim)
    phi_queries = features(queries, rand_feat, temper)
    numer = jnp.einsum("nhm,hme->nhe", phi_queries, kernel_sum, precision=lax.Precision.HIGHEST)
    denom = jnp.einsum("nhm,hm->nh", phi_queries, key_total, precision=lax.Precision.HIGHEST)
    mixed = (
        (local + numer / denom[..., None])
        .astype(jnp.bfloat16)
        .reshape(part_rows, heads_here * head_dim)
    )
    returned = lax.all_to_all(mixed, "head", split_axis=0, concat_axis=1, tiled=True)
    return jnp.dot(returned, w_out, preferred_element_type=jnp.float32).astype(jnp.bfloat16)


def solution(mesh):
    return jax.shard_map(
        shards,
        mesh=mesh,
        in_specs=(
            P(("dom", "head"), None),
            P(),
            P(None, "head"),
            P(),
            P("head", None, None),
            P("head"),
            P("dom", None),
            P("dom"),
            P(),
        ),
        out_specs=P(("dom", "head"), None),
        check_vma=False,
    )
```

profile of v0, /device:TPU:1, one launch (start us, length us, event | category | flops | bytes accessed | tf_op | source)
XLA Modules:
  0.0 337.9 jit_solution(1613953993842794324)
XLA Ops:
  6.5 0.0 all-gather.2.cloned.1.call-start
  6.6 1.1 convert_reduce_fusion
  7.7 1.1 fusion.31
  8.8 1.7 fusion.33
  10.5 0.0 all-gather.2.cloned.1.call-update
  10.5 0.0 all-reduce.2.cloned.1.call-start
  10.6 1.3 compare_and_fusion
  11.8 0.1 reshape.313
  11.9 0.7 compare_select_fusion.1
  12.6 0.1 reshape.298
  12.7 0.8 gather_fusion
  13.5 0.1 reshape.297
  13.6 0.1 copy.20
  14.4 0.1 dynamic_slice.14
  14.5 0.1 select_bitcast_fusion
  14.6 0.1 fusion.44
  14.6 33.0 %all-gather.2.cloned.1.call-done = bf16[1024,512]{1,0:T(8,128)(2,1)} async-done(((bf16[128,512]{1,0:T(8,128)(2,1)}), bf16[1024,512]{1,0:T(8,128)(2,1)}) %all-gather.2.cloned.1.call-update) | async-done | bytes 1048592 | tf_op jit(solution)/shard_map/all_gather | solution.py:51
  47.6 1.7 convolution_convert_fusion
  49.4 3.0 collective-permute-start
  52.4 1.3 collective-permute-start.1
  53.7 0.1 multiply_reduce_fusion
  53.9 1.3 fusion.48
  55.1 1.1 fusion.27
  56.2 1.1 fusion.12
  57.4 0.7 copy.30
  58.1 0.0 all-reduce.2.cloned.1.call-update
  58.1 117.4 %psum.15 = f32[256]{0:T(256)S(1)} all-reduce(f32[256]{0:T(256)S(1)} %get-tuple-element.43), channel_id=1, replica_groups=mesh['dom'=64,'head'=8] {'dom'}, use_global_device_ids=true, to_apply=%region_8.10 | all-reduce | flops 256 | bytes 2048 | tf_op jit(solution)/shard_map/psum | solution.py:67
  175.5 1.0 fusion.49
  176.5 0.0 collective-permute-done.1
  176.5 0.1 maximum_bitcast_fusion
  176.6 0.2 copy.29
  176.7 0.1 fusion.47
  176.8 0.2 copy_bitcast_fusion
  177.0 0.7 gather_fusion.1
  177.7 0.7 gather_fusion.2
  178.4 1.8 broadcast_select_fusion
  180.2 0.6 copy.22
  180.7 0.9 reshape.266
  181.6 1.7 copy.19
  183.3 1.8 reshape.264
  185.1 0.7 fusion
  185.8 0.9 fusion.1
  186.8 1.0 fusion.24
  187.7 0.2 copy.24
  187.9 120.0 %all-reduce.2.cloned.1.call-done = f32[256,64]{0,1:T(8,128)} async-done(((f32[256,64]{0,1:T(8,128)}), f32[256,64]{0,1:T(8,128)}) %all-reduce.2.cloned.1.call-update) | async-done | bytes 65552 | tf_op jit(solution)/shard_map/psum | solution.py:67
  307.9 2.0 fusion.20
  309.9 20.3 %all_to_all.19 = bf16[8,128,64]{1,2,0:T(8,128)(2,1)S(1)} all-to-all(bf16[8,128,64]{1,2,0:T(8,128)(2,1)S(1)} %copy.26), channel_id=1, replica_groups=mesh['dom'=64,'head'=8] {'head'}, dimensions={0} | all-to-all | bytes 262144 | tf_op jit(solution)/shard_map/all_to_all | solution.py:120
  330.2 0.9 convolution_convert_fusion.1
  (29 shorter events, 0.1 us)
Async XLA Ops:
  6.5 323.6 %copy-start = (bf16[512,512]{1,0:T(8,128)(2,1)S(1)}, bf16[512,512]{1,0:T(8,128)(2,1)}, u32[]{:S(2)}) copy-start(bf16[512,512]{1,0:T(8,128)(2,1)} %param.14) | copy-start | bytes 1572868
  6.5 7.1 %copy-start.6 = (s32[8,6]{1,0:T(8,128)S(1)}, s32[8,6]{1,0:T(8,128)}, u32[]{:S(2)}) copy-start(s32[8,6]{1,0:T(8,128)} %param.17) | copy-start | bytes 580
  6.5 6.2 %copy-start.1 = (s32[512]{0:T(512)S(1)}, s32[512]{0:T(512)}, u32[]{:S(2)}) copy-start(s32[512]{0:T(512)} %param.19) | copy-start | bytes 6148
  6.5 8.0 %copy-start.7 = (s32[8]{0:T(128)S(1)}, s32[8]{0:T(128)}, u32[]{:S(2)}) copy-start(s32[8]{0:T(128)} %param.18) | copy-start | bytes 100
  6.5 41.1 %copy-start.5 = (bf16[512,192]{0,1:T(8,128)(2,1)S(1)}, bf16[512,192]{0,1:T(8,128)(2,1)}, u32[]{:S(2)}) copy-start(bf16[512,192]{0,1:T(8,128)(2,1)} %param.13) | copy-start | bytes 589828
  6.5 41.1 %all-gather.2.cloned.1.call-start = ((), (), s32[]{:S(2)}) async-start(), calls=%async_computation.1 | async-start | bytes 1179648 | tf_op jit(solution)/shard_map/all_gather | solution.py:51
  10.5 297.3 %all-reduce.2.cloned.1.call-start = ((), (), s32[]{:S(2)}) async-start(), calls=%async_computation.2 | async-start | bytes 131072 | tf_op jit(solution)/shard_map/psum | solution.py:67
  12.7 41.1 %copy-start.4 = (f32[1,64,256]{2,1,0:T(8,128)S(1)}, f32[1,64,256]{2,1,0:T(8,128)}, u32[]{:S(2)}) copy-start(f32[1,64,256]{2,1,0:T(8,128)} %param.15) | copy-start | bytes 196612
  49.4 127.1 %collective-permute-start = (bf16[1024,128]{0,1:T(8,128)(2,1)S(1)}, bf16[1024,128]{0,1:T(8,128)(2,1)S(1)}, u32[]{:S(2)}, u32[]{:S(2)}) collective-permute-start(bf16[1024,128]{0,1:T(8,128)(2,1)S(1)} %bitcast.148), channel_id=1, source_target_pairs={{0,8},{8,16},{16,24},{24,32},{32,40},{40,48},{48,56},{56,64},{64,7... | collective-permute-start | bytes 786440 | tf_op jit(solution)/shard_map/ppermute | solution.py:15
  52.4 124.1 %collective-permute-start.1 = (bf16[1024,128]{0,1:T(8,128)(2,1)S(1)}, bf16[1024,128]{0,1:T(8,128)(2,1)S(1)}, u32[]{:S(2)}, u32[]{:S(2)}) collective-permute-start(bf16[1024,128]{0,1:T(8,128)(2,1)S(1)} %bitcast.149), channel_id=1, source_target_pairs={{8,0},{16,8},{24,16},{32,24},{40,32},{48,40},{56,48},{64,56},{72,6... | collective-permute-start | bytes 786440 | tf_op jit(solution)/shard_map/ppermute | solution.py:18
  180.7 4.4 %copy-start.3 = (bf16[8,8,8,128]{3,2,1,0:T(8,128)(2,1)S(1)}, bf16[8,8,8,128]{3,2,1,0:T(8,128)(2,1)}, u32[]{:S(2)}) copy-start(bf16[8,8,8,128]{3,2,1,0:T(8,128)(2,1)} %copy.30) | copy-start | bytes 393220
  185.1 1.6 copy-start.2
Sparse Core Ops, SparseCore 0:
  10.6 36.9 all-gather.1
  58.2 249.6 all-reduce.1
where the time goes:
time: 338 us
  waiting for transfers between devices  153 us (45%)
  blocking collectives  138 us (41%)
  between operations  14.4 us (4%)
  matrix products  10.7 us (3%)
  local copies, waits for them, and re-layouts  8.88 us (3%)
  other arithmetic  8.83 us (3%)
  starting transfers between devices  4.4 us (1%)
    psum x1, waiting for transfers between devices, shards(): lax.psum((partial_sum, jnp.sum(phi_keys, axis=0)), 'dom')  120 us
    psum x1, blocking collectives, shards(): lax.psum((partial_sum, jnp.sum(phi_keys, axis=0)), 'dom')  117 us
    all_gather x1, waiting for transfers between devices, shards(): lax.all_gather(normed, 'head', axis=0, tiled=True)  33 us
    all_to_all x1, blocking collectives, shards(): lax.all_to_all(mixed, 'head', split_axis=0, concat_axis=1, tiled=True)  20.3 us
  transfers between devices with their start and end apart: 4, of which 2 were waited for; matrix products, arithmetic and copies ran while one was open for 6% of the time, Pallas kernels for 0%

commit v1 on v0

--- a/solution.py
+++ b/solution.py
@@ -39,6 +39,37 @@
 def shards(
     node_feats, norm_gain, w_qkv, w_out, rand_feat, temper, edge_src, edge_count, block_fill
 ):
+
+    def serve_forms(array_here, group_axis):
+        block_next, right_arr, u1 = (
+            lax.axis_size(group_axis),
+            lax.axis_index(group_axis),
+            array_here.shape[0],
+        )
+        sheets = []
+        for at in tuple(range(block_next)):
+            sheets.append((at, (at + 1) % block_next))
+        grid = []
+        for at in [*range(block_next)]:
+            grid.append((at, (at - 1) % block_next))
+        value_now = jnp.zeros(
+            (*array_here.shape[:0], block_next * u1, *array_here.shape[1:]), array_here.dtype
+        )
+        value_now = lax.dynamic_update_slice_in_dim(value_now, array_here, right_arr * u1, axis=0)
+        o_now = spare = array_here
+        upper = block_next // 2
+        for q in tuple(range(1, upper + 1)):
+            o_now = lax.ppermute(o_now, axis_name=group_axis, perm=sheets)
+            value_now = lax.dynamic_update_slice_in_dim(
+                value_now, o_now, (right_arr - q) % block_next * u1, axis=0
+            )
+            if q < block_next - upper:
+                spare = lax.ppermute(spare, axis_name=group_axis, perm=grid)
+                value_now = lax.dynamic_update_slice_in_dim(
+                    value_now, spare, (right_arr + q) % block_next * u1, axis=0
+                )
+        return value_now
+
     groups = lax.axis_size("head")
     heads_here = rand_feat.shape[0]
     head_dim = rand_feat.shape[1]
@@ -47,11 +78,9 @@
     slots = edge_src.shape[1]
     domain = lax.axis_index("dom")
     normed = layer_norm(node_feats, norm_gain)
-    qkv = jnp.dot(
-        lax.all_gather(normed, "head", axis=0, tiled=True),
-        w_qkv,
-        preferred_element_type=jnp.float32,
-    ).astype(jnp.bfloat16)
+    qkv = jnp.dot(serve_forms(normed, "head"), w_qkv, preferred_element_type=jnp.float32).astype(
+        jnp.bfloat16
+    )
     split = qkv.reshape(part_rows, heads_here, 3, head_dim)
     queries = split[:, :, 0]
     own_fill = lax.dynamic_slice_in_dim(block_fill, domain * blocks, blocks)

time: 338 us -> 327 us (0.967)
  waiting for transfers between devices: 153 us -> 128 us
  starting transfers between devices: 4.4 us -> 17.2 us
    all_gather x1 -> x0, waiting for transfers between devices: 33 us -> none  [shards(): lax.all_gather(normed, 'head', axis=0, tiled=True)]
    ppermute x0 -> x7, starting transfers between devices: none -> 14.6 us  [the longest x3 11.3 us: serve_forms(): spare = lax.ppermute(spare, axis_name=group_axis, perm=grid)]
    ppermute x0 -> x7, waiting for transfers between devices: none -> 7.16 us  [the longest x4 7 us: serve_forms(): o_now = lax.ppermute(o_now, axis_name=group_axis, perm=sheets)]
  transfers between devices with their start and end apart: 4 -> 10, of which waited for: 2 -> 5; matrix products, arithmetic and copies ran while one was open for 6% -> 6% of each run, Pallas kernels for 0% -> 0%
where the time goes in v1:
time: 327 us; the launch traced here: 326 us
  blocking collectives  140 us (43%)
  waiting for transfers between devices  128 us (39%)
  starting transfers between devices  17.2 us (5%)
  between operations  14.5 us (4%)
  matrix products  9.48 us (3%)
  local copies, waits for them, and re-layouts  9.05 us (3%)
  other arithmetic  8.08 us (2%)
    psum x1, waiting for transfers between devices, shards(): lax.psum((partial_sum, jnp.sum(phi_keys, axis=0)), 'dom')  121 us
    psum x1, blocking collectives, shards(): lax.psum((partial_sum, jnp.sum(phi_keys, axis=0)), 'dom')  120 us
    all_to_all x1, blocking collectives, shards(): lax.all_to_all(mixed, 'head', split_axis=0, concat_axis=1, tiled=True)  20.3 us
    ppermute x3, starting transfers between devices, serve_forms(): spare = lax.ppermute(spare, axis_name=group_axis, perm=grid)  11.3 us
    ppermute x4, waiting for transfers between devices, serve_forms(): o_now = lax.ppermute(o_now, axis_name=group_axis, perm=sheets)  7 us
  transfers between devices with their start and end apart: 10, of which 5 were waited for; matrix products, arithmetic and copies ran while one was open for 6% of the time, Pallas kernels for 0%

profile of v1, /device:TPU:1, one launch (start us, length us, event | category | flops | bytes accessed | tf_op | source)
XLA Modules:
  0.0 326.2 jit_solution(827262008892163832)
XLA Ops:
  6.6 1.1 convert_reduce_fusion
  7.7 1.1 fusion.31
  8.8 0.1 broadcast_in_dim.56
  8.8 1.0 constant_dynamic-update-slice_fusion.7
  9.9 2.7 collective-permute-start
  12.6 4.2 %collective-permute-start.1 = (bf16[128,512]{1,0:T(8,128)(2,1)S(1)}, bf16[128,512]{1,0:T(8,128)(2,1)S(1)}, u32[]{:S(2)}, u32[]{:S(2)}) collective-permute-start(bf16[128,512]{1,0:T(8,128)(2,1)S(1)} %get-tuple-element.36), channel_id=1, source_target_pairs={{0,7},{1,0},{2,1},{3,2},{4,3},{5,4},{6,5},{7,6},{8,15},{9,8},{10,9... | collective-permute-start | bytes 393224 | tf_op jit(solution)/shard_map/ppermute | solution.py:67
  16.8 0.7 compare_select_fusion.1
  17.5 1.2 compare_and_fusion
  18.7 0.1 reshape.298
  18.8 0.8 gather_fusion
  19.6 0.1 reshape.297
  19.7 0.1 copy.20
  20.1 0.1 reshape.313
  21.0 2.9 collective-permute-start.3
  24.0 0.8 collective-permute-done.2
  24.7 0.6 collective-permute-start.4
  25.4 4.1 %collective-permute-start.5 = (bf16[128,512]{1,0:T(8,128)(2,1)S(1)}, bf16[128,512]{1,0:T(8,128)(2,1)S(1)}, u32[]{:S(2)}, u32[]{:S(2)}) collective-permute-start(bf16[128,512]{1,0:T(8,128)(2,1)S(1)} %collective-permute-done.3), channel_id=1, source_target_pairs={{0,7},{1,0},{2,1},{3,2},{4,3},{5,4},{6,5},{7,6},{8,15},{9,8},{10,9... | collective-permute-start | bytes 393224 | tf_op jit(solution)/shard_map/ppermute | solution.py:67
  29.5 0.8 collective-permute-done.4
  30.4 0.1 collective-permute-done.5
  30.5 5.4 %collective-permute-done.6 = bf16[128,512]{1,0:T(8,128)(2,1)S(1)} collective-permute-done((bf16[128,512]{1,0:T(8,128)(2,1)S(1)}, bf16[128,512]{1,0:T(8,128)(2,1)S(1)}, u32[]{:S(2)}, u32[]{:S(2)}) %collective-permute-start.6) | collective-permute-done | bytes 131104 | tf_op jit(solution)/shard_map/ppermute | solution.py:62
  36.0 0.5 convolution_convert_fusion
  36.5 1.3 collective-permute-start.7
  37.8 1.3 collective-permute-start.8
  39.1 0.1 multiply_reduce_fusion
  39.3 1.2 fusion.49
  40.5 1.1 fusion.27
  41.6 1.1 fusion.12
  42.8 0.7 copy.30
  43.5 119.8 %psum.15 = f32[256]{0:T(256)S(1)} all-reduce(f32[256]{0:T(256)S(1)} %get-tuple-element.45), channel_id=1, replica_groups=mesh['dom'=64,'head'=8] {'dom'}, use_global_device_ids=true, to_apply=%region_8.10 | all-reduce | flops 256 | bytes 2048 | tf_op jit(solution)/shard_map/psum | solution.py:96
  163.2 1.0 fusion.50
  164.3 0.2 copy.29
  164.4 0.1 fusion.48
  164.5 0.2 copy_bitcast_fusion
  164.7 0.7 gather_fusion.1
  165.4 0.7 gather_fusion.2
  166.1 1.7 broadcast_select_fusion
  167.9 0.6 copy.22
  168.4 0.9 reshape.266
  169.3 1.7 copy.19
  171.0 1.8 reshape.264
  172.8 0.7 fusion
  173.5 0.9 fusion.1
  174.5 1.0 fusion.24
  175.4 0.2 copy.24
  175.6 120.5 %all-reduce.2.cloned.1.call-done = f32[256,64]{0,1:T(8,128)} async-done(((f32[256,64]{0,1:T(8,128)}), f32[256,64]{0,1:T(8,128)}) %all-reduce.2.cloned.1.call-update) | async-done | bytes 65552 | tf_op jit(solution)/shard_map/psum | solution.py:96
  296.1 2.0 fusion.20
  298.2 20.3 %all_to_all.19 = bf16[8,128,64]{1,2,0:T(8,128)(2,1)S(1)} all-to-all(bf16[8,128,64]{1,2,0:T(8,128)(2,1)S(1)} %copy.26), channel_id=1, replica_groups=mesh['dom'=64,'head'=8] {'head'}, dimensions={0} | all-to-all | bytes 262144 | tf_op jit(solution)/shard_map/all_to_all | solution.py:149
  318.5 0.9 convolution_convert_fusion.1
  (48 shorter events, 0.6 us)
Async XLA Ops:
  6.5 311.9 %copy-start = (bf16[512,512]{1,0:T(8,128)(2,1)S(1)}, bf16[512,512]{1,0:T(8,128)(2,1)}, u32[]{:S(2)}) copy-start(bf16[512,512]{1,0:T(8,128)(2,1)} %param.14) | copy-start | bytes 1572868
  6.5 13.2 %copy-start.6 = (s32[8,6]{1,0:T(8,128)S(1)}, s32[8,6]{1,0:T(8,128)}, u32[]{:S(2)}) copy-start(s32[8,6]{1,0:T(8,128)} %param.17) | copy-start | bytes 580
  6.5 12.3 %copy-start.1 = (s32[512]{0:T(512)S(1)}, s32[512]{0:T(512)}, u32[]{:S(2)}) copy-start(s32[512]{0:T(512)} %param.19) | copy-start | bytes 6148
  6.5 13.4 %copy-start.7 = (s32[8]{0:T(128)S(1)}, s32[8]{0:T(128)}, u32[]{:S(2)}) copy-start(s32[8]{0:T(128)} %param.18) | copy-start | bytes 100
  6.5 289.6 %all-reduce.2.cloned.1.call-start = ((), (), s32[]{:S(2)}) async-start(), calls=%async_computation.1 | async-start | bytes 131072 | tf_op jit(solution)/shard_map/psum | solution.py:96
  9.9 11.0 %collective-permute-start = (bf16[128,512]{1,0:T(8,128)(2,1)S(1)}, bf16[128,512]{1,0:T(8,128)(2,1)S(1)}, u32[]{:S(2)}, u32[]{:S(2)}) collective-permute-start(bf16[128,512]{1,0:T(8,128)(2,1)S(1)} %get-tuple-element.36), channel_id=1, source_target_pairs={{0,1},{1,2},{2,3},{3,4},{4,5},{5,6},{6,7},{7,0},{8,9},{9,10},{10,1... | collective-permute-start | bytes 393224 | tf_op jit(solution)/shard_map/ppermute | solution.py:62
  12.6 8.4 %collective-permute-start.1 = (bf16[128,512]{1,0:T(8,128)(2,1)S(1)}, bf16[128,512]{1,0:T(8,128)(2,1)S(1)}, u32[]{:S(2)}, u32[]{:S(2)}) collective-permute-start(bf16[128,512]{1,0:T(8,128)(2,1)S(1)} %get-tuple-element.36), channel_id=1, source_target_pairs={{0,7},{1,0},{2,1},{3,2},{4,3},{5,4},{6,5},{7,6},{8,15},{9,8},{10,9... | collective-permute-start | bytes 393224 | tf_op jit(solution)/shard_map/ppermute | solution.py:67
  18.8 17.1 %copy-start.5 = (bf16[512,192]{0,1:T(8,128)(2,1)S(1)}, bf16[512,192]{0,1:T(8,128)(2,1)}, u32[]{:S(2)}) copy-start(bf16[512,192]{0,1:T(8,128)(2,1)} %param.13) | copy-start | bytes 589828
  19.6 19.6 %copy-start.4 = (f32[1,64,256]{2,1,0:T(8,128)S(1)}, f32[1,64,256]{2,1,0:T(8,128)}, u32[]{:S(2)}) copy-start(f32[1,64,256]{2,1,0:T(8,128)} %param.15) | copy-start | bytes 196612
  20.9 3.8 %collective-permute-start.2 = (bf16[128,512]{1,0:T(8,128)(2,1)S(1)}, bf16[128,512]{1,0:T(8,128)(2,1)S(1)}, u32[]{:S(2)}, u32[]{:S(2)}) collective-permute-start(bf16[128,512]{1,0:T(8,128)(2,1)S(1)} %collective-permute-done), channel_id=1, source_target_pairs={{0,1},{1,2},{2,3},{3,4},{4,5},{5,6},{6,7},{7,0},{8,9},{9,10},{10,1... | collective-permute-start | bytes 393224 | tf_op jit(solution)/shard_map/ppermute | solution.py:62
  21.0 4.4 %collective-permute-start.3 = (bf16[128,512]{1,0:T(8,128)(2,1)S(1)}, bf16[128,512]{1,0:T(8,128)(2,1)S(1)}, u32[]{:S(2)}, u32[]{:S(2)}) collective-permute-start(bf16[128,512]{1,0:T(8,128)(2,1)S(1)} %collective-permute-done.1), channel_id=1, source_target_pairs={{0,7},{1,0},{2,1},{3,2},{4,3},{5,4},{6,5},{7,6},{8,15},{9,8},{10,9... | collective-permute-start | bytes 393224 | tf_op jit(solution)/shard_map/ppermute | solution.py:67
  24.7 5.6 %collective-permute-start.4 = (bf16[128,512]{1,0:T(8,128)(2,1)S(1)}, bf16[128,512]{1,0:T(8,128)(2,1)S(1)}, u32[]{:S(2)}, u32[]{:S(2)}) collective-permute-start(bf16[128,512]{1,0:T(8,128)(2,1)S(1)} %collective-permute-done.2), channel_id=1, source_target_pairs={{0,1},{1,2},{2,3},{3,4},{4,5},{5,6},{6,7},{7,0},{8,9},{9,10},{10,1... | collective-permute-start | bytes 393224 | tf_op jit(solution)/shard_map/ppermute | solution.py:62
  25.4 5.1 %collective-permute-start.5 = (bf16[128,512]{1,0:T(8,128)(2,1)S(1)}, bf16[128,512]{1,0:T(8,128)(2,1)S(1)}, u32[]{:S(2)}, u32[]{:S(2)}) collective-permute-start(bf16[128,512]{1,0:T(8,128)(2,1)S(1)} %collective-permute-done.3), channel_id=1, source_target_pairs={{0,7},{1,0},{2,1},{3,2},{4,3},{5,4},{6,5},{7,6},{8,15},{9,8},{10,9... | collective-permute-start | bytes 393224 | tf_op jit(solution)/shard_map/ppermute | solution.py:67
  30.3 5.6 %collective-permute-start.6 = (bf16[128,512]{1,0:T(8,128)(2,1)S(1)}, bf16[128,512]{1,0:T(8,128)(2,1)S(1)}, u32[]{:S(2)}, u32[]{:S(2)}) collective-permute-start(bf16[128,512]{1,0:T(8,128)(2,1)S(1)} %collective-permute-done.4), channel_id=1, source_target_pairs={{0,1},{1,2},{2,3},{3,4},{4,5},{5,6},{6,7},{7,0},{8,9},{9,10},{10,1... | collective-permute-start | bytes 393224 | tf_op jit(solution)/shard_map/ppermute | solution.py:62
  36.5 127.7 %collective-permute-start.7 = (bf16[1024,128]{0,1:T(8,128)(2,1)S(1)}, bf16[1024,128]{0,1:T(8,128)(2,1)S(1)}, u32[]{:S(2)}, u32[]{:S(2)}) collective-permute-start(bf16[1024,128]{0,1:T(8,128)(2,1)S(1)} %bitcast.148), channel_id=1, source_target_pairs={{0,8},{8,16},{16,24},{24,32},{32,40},{40,48},{48,56},{56,64},{64,7... | collective-permute-start | bytes 786440 | tf_op jit(solution)/shard_map/ppermute | solution.py:15
  37.8 126.4 %collective-permute-start.8 = (bf16[1024,128]{0,1:T(8,128)(2,1)S(1)}, bf16[1024,128]{0,1:T(8,128)(2,1)S(1)}, u32[]{:S(2)}, u32[]{:S(2)}) collective-permute-start(bf16[1024,128]{0,1:T(8,128)(2,1)S(1)} %bitcast.149), channel_id=1, source_target_pairs={{8,0},{16,8},{24,16},{32,24},{40,32},{48,40},{56,48},{64,56},{72,6... | collective-permute-start | bytes 786440 | tf_op jit(solution)/shard_map/ppermute | solution.py:18
  168.4 4.4 %copy-start.3 = (bf16[8,8,8,128]{3,2,1,0:T(8,128)(2,1)S(1)}, bf16[8,8,8,128]{3,2,1,0:T(8,128)(2,1)}, u32[]{:S(2)}) copy-start(bf16[8,8,8,128]{3,2,1,0:T(8,128)(2,1)} %copy.30) | copy-start | bytes 393220
  172.8 1.6 copy-start.2
Sparse Core Ops, SparseCore 0:
  43.6 252.5 all-reduce.1
